TPU v7x, 32 devices: a whole 2x2x4 slice. The times are simulated.
32 devices in a mesh: section: 8 (over z, core), tensor: 4 (over y, x).
Axes of the slice: x: 2, y: 2, z: 4, core: 2. Of those that a mesh axis runs over, the one named last changes fastest.
Arguments:
- activations: bfloat16 [8, 512, 4096], P('section', None, 'tensor'), may hold values from -48 to 48
- gain: bfloat16 [8, 4096], P('section', 'tensor'), may hold values from 0.5 to 1.5
- w_query: bfloat16 [8, 4096, 4096], P('section', None, 'tensor'), may hold values from -0.0625 to 0.0625
- w_kv: bfloat16 [8, 1024, 4096], P('section', 'tensor'), may hold values from -1.8782524 to 1.8782524
- segments: int32 [8, 512], replicated, may hold values from 0 to 31, never falling along the last dimension, each value on 1 to 128 neighbouring positions
- pool: bfloat16 [16, 128, 4096], P('section', None, 'tensor'), may hold values from -48 to 48
- row_ids: int32 [32], replicated, may hold values from 0 to 15, as said below
- row_lengths: int32 [32], replicated, may hold values from 1 to 128, 512 in all
Outputs:
- after_first: bfloat16 [8, 512, 4096], P('section', None, 'tensor')
- after_second: bfloat16 [8, 512, 4096], P('section', None, 'tensor')
Inputs may be any that keep to these rules, and one draw needn't show every extreme that they name: `row_ids`: every block of 2 consecutive ids, the rows of one buffer host, is named at least once; ids may repeat.
All inputs are finite; a program needn't handle non-finite values.
Results may differ from a plain program's by a relative error of at most 0.01.
Values may be sent and summed in bfloat16 or wider, within the bound.
A program may use at most 64 MiB of HBM per device.

v0:
```python
import jax
import jax.numpy as jnp
from jax import lax
from jax.sharding import PartitionSpec as P

D = 4096
HEADS = 32
KV_HEADS = 4
HEAD_DIM = 128


norm_eps = 1e-05
masked_score = -1e30


def partner_2(block, axis, distance):
    count = lax.axis_size(axis)
    route = []
    for low in range(count):
        high = low | 1 << distance
        if high != low and high < count:
            route += [(low, high), (high, low)]
    return lax.ppermute(block, axis, route)


def from_behind(block, axis, distance):
    devices = range(lax.axis_size(axis))
    route = [(i - distance, i) for i in devices if i - distance in devices]
    return lax.ppermute(block, axis, route)


def attend(inputs, gain_cols, query_weight, keyval_weight, seg_ids, tensor_index):
    row_count, col_count = inputs.shape
    wide_inputs = inputs.astype(jnp.float32)
    square_total = lax.psum(jnp.sum(wide_inputs * wide_inputs, axis=1), "tensor")
    row_scale = lax.rsqrt(square_total / D + norm_eps)
    normed = (wide_inputs * row_scale[:, None] * gain_cols.astype(jnp.float32)[None, :]).astype(
        jnp.bfloat16
    )
    part_cols = lax.all_gather(normed, "tensor", axis=1, tiled=True)
    query_part = jnp.dot(part_cols, query_weight, preferred_element_type=jnp.float32)
    keyval_part = lax.dot_general(
        keyval_weight, part_cols, (((1,), (1,)), ((), ())), preferred_element_type=jnp.float32
    )
    query = query_part.astype(jnp.bfloat16)
    keyval = keyval_part.astype(jnp.bfloat16)
    heads_here = query_weight.shape[1] // HEAD_DIM
    group_size = HEADS // KV_HEADS
    group_devices = group_size // heads_here
    head_block = keyval
    for bit_number in range(group_devices.bit_length() - 1):
        partner = partner_2(head_block, "tensor", bit_number)
        is_lower = tensor_index // (1 << bit_number) % 2 == 0
        head_block = jnp.where(
            is_lower,
            jnp.concatenate([head_block, partner], axis=0),
            jnp.concatenate([partner, head_block], axis=0),
        )
    keys_cols = head_block[:HEAD_DIM]
    values_cols = head_block[HEAD_DIM:]
    query_heads = query.reshape(row_count, heads_here, HEAD_DIM)
    scores = jnp.einsum(
        "rhd,ds->hrs", query_heads, keys_cols, preferred_element_type=jnp.float32
    ) * HEAD_DIM ** (-0.5)
    positions = jnp.arange(row_count, dtype=jnp.int32)
    allowed = (seg_ids[:, None] == seg_ids[None, :]) & (positions[None, :] <= positions[:, None])
    scores = jnp.where(allowed[None, :, :], scores, masked_score)
    weights = jax.nn.softmax(scores, axis=-1).astype(jnp.bfloat16)
    context = jnp.einsum("hrs,ds->rhd", weights, values_cols, preferred_element_type=jnp.float32)
    context = context.astype(jnp.bfloat16).reshape(row_count, col_count)
    return (wide_inputs + context.astype(jnp.float32)).astype(jnp.bfloat16)


def pick_rows(running, host_rows, source):
    flat_rows = host_rows.reshape(-1, host_rows.shape[2])
    inside = (source >= 0) & (source < flat_rows.shape[0])
    taken = jnp.take(flat_rows, jnp.clip(source, 0, flat_rows.shape[0] - 1), axis=0)
    return jnp.where(inside[:, None], taken, running)


def per_device(activations, gain, w_query, w_kv, segments, pool, row_ids, row_lengths):
    section_index = lax.axis_index("section")
    tensor_index = lax.axis_index("tensor")
    token_count = activations.shape[1]
    col_count = activations.shape[2]
    own_segments = lax.dynamic_index_in_dim(segments, section_index, 0, keepdims=False)
    after_first = attend(activations[0], gain[0], w_query[0], w_kv[0], own_segments, tensor_index)[
        None
    ]
    ends = jnp.cumsum(row_lengths)
    positions = jnp.arange(token_count, dtype=jnp.int32)
    slot = jnp.sum((positions[:, None] >= ends[None, :]).astype(jnp.int32), axis=1)
    slot_match = slot[:, None] == jnp.arange(row_ids.shape[0], dtype=jnp.int32)[None, :]
    slot_start = jnp.sum(jnp.where(slot_match, (ends - row_lengths)[None, :], 0), axis=1)
    slot_row = jnp.sum(jnp.where(slot_match, row_ids[None, :], 0), axis=1)
    source = slot_row * pool.shape[1] + positions - slot_start
    empty_rows = jnp.zeros((token_count, col_count), jnp.bfloat16)
    fresh = pick_rows(empty_rows, lax.all_gather(pool, "section", axis=0, tiled=True), source)
    handed = from_behind(after_first, "section", 1)
    second_inputs = jnp.where(section_index == 0, fresh[None], handed)
    prior_segments = lax.dynamic_index_in_dim(
        segments, jnp.maximum(section_index - 1, 0), 0, keepdims=False
    )
    second_segments = jnp.where(section_index == 0, slot, prior_segments)
    after_second = attend(
        second_inputs[0], gain[0], w_query[0], w_kv[0], second_segments, tensor_index
    )[None]
    return (after_first, after_second)


def solution(mesh):
    return jax.shard_map(
        per_device,
        mesh=mesh,
        in_specs=(
            P("section", None, "tensor"),
            P("section", "tensor"),
            P("section", None, "tensor"),
            P("section", "tensor", None),
            P(),
            P("section", None, "tensor"),
            P(),
            P(),
        ),
        out_specs=(P("section", None, "tensor"), P("section", None, "tensor")),
        check_vma=False,
    )
```

profile of v0, /device:TPU:0, one launch (start us, length us, event | category | flops | bytes accessed | tf_op | source)
XLA Modules:
  0.0 234.6 jit_solution(6487976549945096707)
XLA Ops:
  7.2 1.6 fusion.20
  8.9 11.4 %psum.14 = f32[512]{0:T(512)S(1)} all-reduce(f32[512]{0:T(512)S(1)} %fusion.20), channel_id=1, replica_groups=mesh['section'=8,'tensor'=4] {'tensor'}, use_global_device_ids=true, to_apply=%region_1.2 | all-reduce | flops 512 | bytes 4096 | tf_op jit(solution)/shard_map/psum | solution.py:35
  20.9 2.5 %fusion.22 = bf16[512,1024]{1,0:T(8,128)(2,1)} fusion(bf16[1,512,1024]{2,1,0:T(8,128)(2,1)} %param.8, f32[1024]{0:T(1024)S(1)} %bitcast.128, f32[512]{0:T(512)S(1)} %add_rsqrt_fusion.1), kind=kLoop, calls=%fused_computation.33 | loop fusion | flops 2097152 | bytes 2103296 | tf_op jit(solution)/shard_map/convert_element_type | solution.py:37
  25.7 50.0 %all-gather.4.cloned.1.call-done = bf16[512,4096]{1,0:T(8,128)(2,1)} async-done(((bf16[512,1024]{1,0:T(8,128)(2,1)}), bf16[512,4096]{1,0:T(8,128)(2,1)}) %all-gather.4.cloned.1.call-update) | async-done | bytes 4194320 | tf_op jit(solution)/shard_map/all_gather | solution.py:40
  75.7 3.6 %fusion.57 = bf16[256,512]{0,1:T(8,128)(2,1)S(1)} fusion(bf16[512,4096]{1,0:T(8,128)(2,1)} %all-gather.4.cloned.1.call-done, bf16[1,256,4096]{2,1,0:T(8,128)(2,1)S(1)} %copy-done), kind=kOutput, calls=%fused_computation.54 | convolution fusion | flops 1073872896 | bytes 6553600 | tf_op jit(solution)/shard_map/dot_general | solution.py:42
  79.3 7.1 %fusion.45 = bf16[64,8,8,128]{3,2,1,0:T(8,128)(2,1)S(1)} fusion(bf16[512,4096]{1,0:T(8,128)(2,1)S(1)} %copy-done.6, bf16[1,4096,1024]{2,1,0:T(8,128)(2,1)} %param.10), kind=kOutput, calls=%fused_computation.50 | convolution fusion | flops 4295491584 | bytes 13631488 | tf_op jit(solution)/shard_map/dot_general | solution.py:41
  86.4 1.3 fusion.63
  87.7 5.7 %fusion.75 = (f32[8,512]{1,0:T(8,128)S(1)}, f32[8,512,512]{1,2,0:T(8,128)}) fusion(f32[512,512,8]{1,0,2:T(8,128)S(1)} %fusion.63, pred[512,512]{0,1:T(8,128)(4,1)S(1)} %fusion.69), kind=kOutput, calls=%fused_computation.93 | output fusion | flops 12583423 | bytes 17055744 | tf_op jit(solution)/shard_map/sub | solution.py:68
  93.4 5.5 %fusion.35 = f32[128,8,512]{2,0,1:T(8,128)} fusion(f32[8,512,512]{1,2,0:T(8,128)} %get-tuple-element.12, f32[8,512]{1,0:T(8,128)S(1)} %get-tuple-element.11, bf16[256,512]{0,1:T(8,128)(2,1)S(1)} %fusion.57), kind=kOutput, calls=%fused_computation.46 | convolution fusion | flops 542113792 | bytes 10633216 | tf_op jit(solution)/shard_map/hrs,ds->rhd/dot_general | solution.py:69
  98.9 3.0 %copy.40 = f32[1,512,1024]{2,1,0:T(8,128)} copy(f32[1,512,1024]{1,2,0:T(8,128)} %bitcast.126) | data formatting | bytes 4194304 | tf_op jit(solution)/shard_map/convert_element_type | solution.py:71
  102.0 2.9 %fusion.23 = bf16[1,512,1024]{2,1,0:T(8,128)(2,1)} fusion(f32[1,512,1024]{2,1,0:T(8,128)} %copy.40, bf16[1,512,1024]{2,1,0:T(8,128)(2,1)S(1)} %copy-done.2), kind=kLoop, calls=%fused_computation.34 | loop fusion | flops 1572864 | bytes 4194304 | tf_op jit(solution)/shard_map/convert_element_type | solution.py:71
  104.9 1.8 collective-permute-start
  106.9 18.1 %all-gather.6.cloned.1.call-done = bf16[16,128,1024]{2,1,0:T(8,128)(2,1)} async-done(((bf16[2,128,1024]{2,1,0:T(8,128)(2,1)}), bf16[16,128,1024]{2,1,0:T(8,128)(2,1)}) %all-gather.6.cloned.1.call-update) | async-done | bytes 4194320 | tf_op jit(solution)/shard_map/all_gather | solution.py:98
  125.0 6.2 %gather_fusion = bf16[512,1024]{1,0:T(8,128)(2,1)} fusion(bf16[2048,1024]{1,0:T(8,128)(2,1)} %bitcast.125, s32[1024]{0:T(1024)S(1)} %pad_clamp_fusion), kind=kCustom, calls=%fused_computation | custom fusion | bytes 2099200 | tf_op jit(solution)/shard_map/jit(_take)/gather | solution.py:77
  132.2 2.0 fusion.24
  134.1 10.5 %psum.15 = f32[512]{0:T(512)S(1)} all-reduce(f32[512]{0:T(512)S(1)} %get-tuple-element.6), channel_id=1, replica_groups=mesh['section'=8,'tensor'=4] {'tensor'}, use_global_device_ids=true, to_apply=%region_9.10 | all-reduce | flops 512 | bytes 4096 | tf_op jit(solution)/shard_map/psum | solution.py:35
  144.7 1.3 fusion.26
  146.2 52.6 %all-gather.8.cloned.1.call-done = bf16[512,4096]{1,0:T(8,128)(2,1)} async-done(((bf16[512,1024]{1,0:T(8,128)(2,1)}), bf16[512,4096]{1,0:T(8,128)(2,1)}) %all-gather.8.cloned.1.call-update) | async-done | bytes 4194320 | tf_op jit(solution)/shard_map/all_gather | solution.py:40
  198.8 3.6 %fusion.54 = bf16[256,512]{0,1:T(8,128)(2,1)S(1)} fusion(bf16[512,4096]{1,0:T(8,128)(2,1)} %all-gather.8.cloned.1.call-done, bf16[1,256,4096]{2,1,0:T(8,128)(2,1)S(1)} %copy-done), kind=kOutput, calls=%fused_computation.53 | convolution fusion | flops 1073872896 | bytes 6553600 | tf_op jit(solution)/shard_map/dot_general | solution.py:42
  202.5 7.1 %fusion.42 = bf16[64,8,8,128]{3,2,1,0:T(8,128)(2,1)S(1)} fusion(bf16[512,4096]{1,0:T(8,128)(2,1)S(1)} %copy-done.7, bf16[1,4096,1024]{2,1,0:T(8,128)(2,1)} %param.10), kind=kOutput, calls=%fused_computation.49 | convolution fusion | flops 4295491584 | bytes 13631488 | tf_op jit(solution)/shard_map/dot_general | solution.py:41
  210.8 5.7 %fusion.76 = (f32[8,512]{1,0:T(8,128)S(1)}, f32[8,512,512]{1,2,0:T(8,128)}) fusion(f32[512,512,8]{1,0,2:T(8,128)S(1)} %fusion.60, pred[512,512]{0,1:T(8,128)(4,1)S(1)} %fusion.68), kind=kOutput, calls=%fused_computation.94 | output fusion | flops 12583423 | bytes 17055744 | tf_op jit(solution)/shard_map/sub | solution.py:68
  216.5 5.5 %fusion.33 = f32[128,8,512]{2,0,1:T(8,128)} fusion(f32[8,512,512]{1,2,0:T(8,128)} %get-tuple-element.14, f32[8,512]{1,0:T(8,128)S(1)} %get-tuple-element.13, bf16[256,512]{0,1:T(8,128)(2,1)S(1)} %fusion.54), kind=kOutput, calls=%fused_computation.44 | convolution fusion | flops 542113792 | bytes 10633216 | tf_op jit(solution)/shard_map/hrs,ds->rhd/dot_general | solution.py:69
  222.1 3.1 %copy.45 = f32[1,512,1024]{2,1,0:T(8,128)} copy(f32[1,512,1024]{1,2,0:T(8,128)} %bitcast.127) | data formatting | bytes 4194304 | tf_op jit(solution)/shard_map/convert_element_type | solution.py:71
  225.2 2.9 %fusion.27 = bf16[1,512,1024]{2,1,0:T(8,128)(2,1)} fusion(f32[1,512,1024]{2,1,0:T(8,128)} %copy.45, bf16[1,512,1024]{2,1,0:T(8,128)(2,1)S(1)} %get-tuple-element.7), kind=kLoop, calls=%fused_computation.38 | loop fusion | flops 1572864 | bytes 4194304 | tf_op jit(solution)/shard_map/convert_element_type | solution.py:71
  (41 shorter events, 5.5 us)
Async XLA Ops:
  7.2 68.5 %copy-start = (bf16[1,256,4096]{2,1,0:T(8,128)(2,1)S(1)}, bf16[1,256,4096]{2,1,0:T(8,128)(2,1)}, u32[]{:S(2)}) copy-start(bf16[1,256,4096]{2,1,0:T(8,128)(2,1)} %param.11) | copy-start | bytes 6291460
  7.2 17.1 %copy-start.5 = (s32[32]{0:T(128)S(1)}, s32[32]{0:T(128)}, u32[]{:S(2)}) copy-start(s32[32]{0:T(128)} %param.15) | copy-start | bytes 388
  7.2 68.5 %all-gather.4.cloned.1.call-start = ((), (), s32[]{:S(2)}) async-start(), calls=%async_computation | async-start | bytes 5242880 | tf_op jit(solution)/shard_map/all_gather | solution.py:40
  23.5 101.5 %all-gather.6.cloned.1.call-start = ((), (), s32[]{:S(2)}) async-start(), calls=%async_computation.1 | async-start | bytes 4718592 | tf_op jit(solution)/shard_map/all_gather | solution.py:98
  24.2 174.6 %all-gather.8.cloned.1.call-start = ((), (), s32[]{:S(2)}) async-start(), calls=%async_computation.2 | async-start | bytes 5242880 | tf_op jit(solution)/shard_map/all_gather | solution.py:40
  75.7 3.6 %copy-start.6 = (bf16[512,4096]{1,0:T(8,128)(2,1)S(1)}, bf16[512,4096]{1,0:T(8,128)(2,1)}, u32[]{:S(2)}) copy-start(bf16[512,4096]{1,0:T(8,128)(2,1)} %all-gather.4.cloned.1.call-done) | copy-start | bytes 12582916
  98.9 3.0 %copy-start.2 = (bf16[1,512,1024]{2,1,0:T(8,128)(2,1)S(1)}, bf16[1,512,1024]{2,1,0:T(8,128)(2,1)}, u32[]{:S(2)}) copy-start(bf16[1,512,1024]{2,1,0:T(8,128)(2,1)} %param.8) | copy-start | bytes 3145732
  98.9 7.8 %copy-start.4 = (s32[32]{0:T(128)S(1)}, s32[32]{0:T(128)}, u32[]{:S(2)}) copy-start(s32[32]{0:T(128)} %param.14) | copy-start | bytes 388
  104.9 26.3 %collective-permute-start = (bf16[1,512,1024]{2,1,0:T(8,128)(2,1)}, bf16[1,512,1024]{2,1,0:T(8,128)(2,1)S(1)}, u32[]{:S(2)}, u32[]{:S(2)}) collective-permute-start(bf16[1,512,1024]{2,1,0:T(8,128)(2,1)} %fusion.23), channel_id=1, source_target_pairs={{0,4},{4,8},{8,12},{12,16},{16,20},{20,24},{24,28},{1,5},{5,9},{9,... | collective-permute-start | bytes 3145736 | tf_op jit(solution)/shard_map/ppermute | solution.py:29
  131.2 1.0 copy-start.3
  198.8 3.6 %copy-start.7 = (bf16[512,4096]{1,0:T(8,128)(2,1)S(1)}, bf16[512,4096]{1,0:T(8,128)(2,1)}, u32[]{:S(2)}) copy-start(bf16[512,4096]{1,0:T(8,128)(2,1)} %all-gather.8.cloned.1.call-done) | copy-start | bytes 12582916
  222.1 6.0 %copy-start.1 = (bf16[1,256,4096]{2,1,0:T(8,128)(2,1)S(1)}, bf16[1,256,4096]{2,1,0:T(8,128)(2,1)}, u32[]{:S(2)}) copy-start(bf16[1,256,4096]{2,1,0:T(8,128)(2,1)} %param.11) | copy-start | bytes 6291460
Sparse Core Ops, SparseCore 0:
  23.6 52.0 all-gather.3
  77.3 47.6 all-gather.5
  146.1 52.7 all-gather.7
where the time goes:
time: 235 us
  waiting for transfers between devices  121 us (51%)
  matrix products  35 us (15%)
  other arithmetic  27 us (11%)
  blocking collectives  21.9 us (9%)
  between operations  13.9 us (6%)
  local copies, waits for them, and re-layouts  13.4 us (6%)
    all_gather x2, waiting for transfers between devices, attend(): part_cols = lax.all_gather(normed, 'tensor', axis=1, tiled=True)  103 us
    psum x2, blocking collectives, attend(): lax.psum(jnp.sum(wide_inputs * wide_inputs, axis=1), 'tensor')  21.9 us
    all_gather x1, waiting for transfers between devices, per_device(): lax.all_gather(pool, 'section', axis=0, tiled=True)  18.1 us
    dot_general x2, matrix products, attend(): jnp.dot(part_cols, query_weight, preferred_element_type=jnp.float32)  14.1 us
    sub x2, other arithmetic, attend(): weights = jax.nn.softmax(scores, axis=-1).astype(jnp.bfloat16)  11.4 us
    dot_general x2, matrix products, attend(): jnp.einsum('hrs,ds->rhd', weights, values_cols, preferred_element_type=jn...  11.1 us
    dot_general x2, matrix products, attend(): lax.dot_general(keyval_weight, part_cols, (((1,), (1,)), ((), ())), prefe...  7.25 us
    gather x1, local copies, waits for them, and re-layouts, pick_rows(): jnp.take(flat_rows, jnp.clip(source, 0, flat_rows.shape[0] - 1), axis=0)  6.21 us
  transfers between devices with their start and end apart: 4, of which 3 were waited for; matrix products, arithmetic and copies ran while one was open for 16% of the time, Pallas kernels for 0%

commit v1 on v0

--- a/solution.py
+++ b/solution.py
@@ -1,6 +1,10 @@
+import functools
+
 import jax
 import jax.numpy as jnp
 from jax import lax
+from jax.experimental import pallas as pl
+from jax.experimental.pallas import tpu as pltpu
 from jax.sharding import PartitionSpec as P
 
 D = 4096
@@ -108,9 +112,389 @@
     return (after_first, after_second)
 
 
+BLOCK = 128
+MESH = pl.DeviceIdType.MESH
+
+
+def relay_kernel(
+    sections, hosts_rows, slots,
+    a_ref, gain_ref, wq_ref, wkv_ref, seg_ref, pool_ref, ids_ref, len_ref,
+    out1_ref, out2_ref,
+    got, weight, kv_raw, gains, normed, query, keys, values, seg_rows, src_rows,
+    pool_rows, above, below, result,
+    own_send, own_recv, fwd_send, fwd_recv, gain_send, gain_recv, hand_send, hand_recv,
+    x_sem, wq_sem, wkv_sem, pool_sem, mate_send, mate_recv, sum_send, sum_recv, out_sem,
+):
+    sec = lax.axis_index("section")
+    ten = lax.axis_index("tensor")
+    blocks = a_ref.shape[1] // BLOCK
+    steps = 2 * blocks
+    cols = a_ref.shape[2]
+    over_x = ten + 1 - 2 * (ten % 2)
+    over_y = ten + 2 - 4 * (ten // 2)
+    peers = (ten, over_x, over_y, 3 - ten)
+    even = sec % 2 == 0
+    top = sections - 2
+
+    x_copies = [
+        pltpu.make_async_copy(
+            a_ref.at[0, pl.ds(k * BLOCK, BLOCK)], got.at[k, 0], x_sem.at[k]
+        )
+        for k in range(blocks)
+    ]
+    wq_copies, wkv_copies = [], []
+    for r in range(4):
+        part = pl.ds(pl.multiple_of(peers[r] * cols, cols), cols)
+        wq_copies.append(
+            pltpu.make_async_copy(
+                wq_ref.at[0, part], weight.at[pl.ds(r * cols, cols), pl.ds(0, cols)], wq_sem.at[r]
+            )
+        )
+        wkv_copies.append(
+            pltpu.make_async_copy(wkv_ref.at[0, :, part], kv_raw.at[r], wkv_sem.at[r])
+        )
+    pool_copy = pltpu.make_async_copy(pool_ref, pool_rows.at[0], pool_sem)
+    x_copies[0].start()
+    for copy in wkv_copies + wq_copies + x_copies[1:]:
+        copy.start()
+
+    @pl.when(even)
+    def _():
+        pool_copy.start()
+
+    barrier = pltpu.get_barrier_semaphore()
+    for r in (1, 2, 3):
+        pl.semaphore_signal(barrier, inc=1, device_id=(sec, peers[r]), device_id_type=MESH)
+
+    def greet(condition, other):
+        @pl.when(condition)
+        def _():
+            pl.semaphore_signal(barrier, inc=1, device_id=(other, ten), device_id_type=MESH)
+
+    greet(sec > 0, sec - 1)
+    greet(sec < sections - 1, sec + 1)
+    greet(even & (sec > 1), sec - 2)
+    greet(even & (sec < top), sec + 2)
+    others = 3
+    for condition in (sec > 0, sec < sections - 1, even & (sec > 1), even & (sec < top)):
+        others = others + jnp.where(condition, 1, 0)
+    pl.semaphore_wait(barrier, others)
+
+    def remote(src, dst, send_sem, recv_sem, device):
+        return pltpu.make_async_remote_copy(
+            src_ref=src, dst_ref=dst, send_sem=send_sem, recv_sem=recv_sem,
+            device_id=device, device_id_type=MESH,
+        )
+
+    def own_copy(src, b, way):
+        return remote(
+            src, got.at[b, 1 + way], own_send.at[b, way], own_recv.at[b, way],
+            (sec, peers[1 + way]),
+        )
+
+    half = BLOCK // 2
+
+    def forward_copy(b, way):
+        rows = pl.ds(way * half, half)
+        return remote(
+            got.at[b, 1 + way, rows], got.at[b, 3, rows], fwd_send.at[b, way],
+            fwd_recv.at[b, way], (sec, peers[2 - way]),
+        )
+
+    def hand_copy(k):
+        return remote(
+            result.at[k], got.at[blocks + k, 0], hand_send.at[k], hand_recv.at[k], (sec + 1, ten)
+        )
+
+    def sum_copy(k):
+        return remote(below.at[k], above.at[k], sum_send.at[k], sum_recv.at[k], (sec - 2, ten))
+
+    def gain_copy(r):
+        return remote(
+            gains.at[0], gains.at[r], gain_send.at[r - 1], gain_recv.at[r - 1], (sec, peers[r])
+        )
+
+    mate_copy = remote(pool_ref, pool_rows.at[1], mate_send, mate_recv, (sec - 1, ten))
+
+    for k in range(2):
+        for way in range(2):
+            own_copy(a_ref.at[0, pl.ds(k * BLOCK, BLOCK)], k, way).start()
+    gains[0] = jnp.broadcast_to(gain_ref[...], gains.shape[1:])
+    for r in (1, 2, 3):
+        gain_copy(r).start()
+
+    @pl.when(sec % 2 == 1)
+    def _():
+        mate_copy.start()
+
+    positions = lax.broadcasted_iota(jnp.int32, (1, blocks * BLOCK), 1)
+    start = jnp.int32(0)
+    slot = jnp.zeros_like(positions)
+    source = jnp.zeros_like(positions)
+    for j in range(slots):
+        here = positions >= start
+        slot = jnp.where(here, j, slot)
+        source = jnp.where(here, ids_ref[j] * pool_ref.shape[1] - start + positions, source)
+        start = start + len_ref[j]
+    first_segments = seg_ref[pl.ds(sec, 1), :]
+    prior_segments = seg_ref[pl.ds(jnp.maximum(sec - 1, 0), 1), :]
+    second_segments = jnp.where(sec == 0, slot, prior_segments)
+    for k in range(blocks):
+        part = slice(k * BLOCK, (k + 1) * BLOCK)
+        seg_rows[k] = first_segments[:, part]
+        seg_rows[blocks + k] = second_segments[:, part]
+        src_rows[k] = source[:, part] - sec * hosts_rows
+    keys[...] = jnp.zeros_like(keys)
+    values[...] = jnp.zeros_like(values)
+
+    def picked(k):
+        index = lax.broadcasted_iota(jnp.int32, (2 * hosts_rows, BLOCK), 0)
+        hit = (index == src_rows[k]).astype(jnp.float32).astype(jnp.bfloat16)
+        rows = pool_rows[...].reshape(2 * hosts_rows, cols)
+        return lax.dot_general(
+            hit, rows, (((0,), (0,)), ((), ())), preferred_element_type=jnp.float32
+        )
+
+    def pass_down(k):
+        sum_copy(k).wait_recv()
+        below[k] = (picked(k) + above[k].astype(jnp.float32)).astype(jnp.bfloat16)
+        sum_copy(k).start()
+
+    middle = even & (sec > 0) & (sec < top)
+
+    @pl.when(even)
+    def _():
+        pool_copy.wait()
+        mate_copy.wait_recv()
+
+        @pl.when(sec == top)
+        def _():
+            def send(k, carry):
+                below[k] = picked(k).astype(jnp.bfloat16)
+                sum_copy(k).start()
+                return carry
+
+            lax.fori_loop(0, blocks, send, 0)
+
+    for r in range(4):
+        wkv_copies[r].wait()
+        weight[r * cols:(r + 1) * cols, cols:] = kv_raw[r].T
+
+    @pl.when(middle)
+    def _():
+        pass_down(0)
+
+    late = jnp.minimum((top - sec) // 2, 2) - 1
+
+    for copy in wq_copies:
+        copy.wait()
+    for r in (1, 2, 3):
+        gain_copy(r).wait_recv()
+
+    def forward(b):
+        for way in range(2):
+            own_copy(got.at[b, 0], b, way).wait_recv()
+            forward_copy(b, way).start()
+
+    forward(0)
+
+    def step(b, carry):
+        ahead = b + 2
+
+        @pl.when(ahead < blocks)
+        def _():
+            for way in range(2):
+                own_copy(
+                    a_ref.at[0, pl.ds(pl.multiple_of(ahead * BLOCK, BLOCK), BLOCK)], ahead, way
+                ).start()
+
+        @pl.when((ahead >= blocks) & (ahead < steps))
+        def _():
+            k = ahead - blocks
+
+            @pl.when(sec > 0)
+            def _():
+                hand_copy(k).wait_recv()
+
+            @pl.when(sec == 0)
+            def _():
+                sum_copy(k).wait_recv()
+                got[ahead, 0] = (picked(k) + above[k].astype(jnp.float32)).astype(jnp.bfloat16)
+
+            for way in range(2):
+                own_copy(got.at[ahead, 0], ahead, way).start()
+
+        @pl.when(b + 1 < steps)
+        def _():
+            forward(b + 1)
+
+        for way in range(2):
+            forward_copy(b, way).wait_recv()
+
+        @pl.when(b < blocks)
+        def _():
+            pltpu.make_async_copy(
+                a_ref.at[0, pl.ds(0, BLOCK)], got.at[b, 0], x_sem.at[b]
+            ).wait()
+
+        total = jnp.zeros((BLOCK, 1), jnp.float32)
+        for r in range(4):
+            wide = got[b, r].astype(jnp.float32)
+            total = total + jnp.sum(wide * wide, axis=1, keepdims=True)
+        scale = lax.rsqrt(total / D + norm_eps)
+        for r in range(4):
+            wide = got[b, r].astype(jnp.float32)
+            gain_row = gains[r].astype(jnp.float32)[0:1]
+            normed[:, r * cols:(r + 1) * cols] = (wide * scale * gain_row).astype(jnp.bfloat16)
+
+        def project(low, width):
+            return jnp.dot(
+                normed[...], weight[:, low:low + width], preferred_element_type=jnp.float32
+            ).astype(jnp.bfloat16)
+
+        keys[0:BLOCK] = keys[BLOCK:]
+        values[0:BLOCK] = values[BLOCK:]
+        keyval = project(cols, 2 * HEAD_DIM)
+        keys[BLOCK:] = keyval[:, :HEAD_DIM]
+        values[BLOCK:] = keyval[:, HEAD_DIM:]
+        for low in range(0, cols, 256):
+            query[:, low:low + 256] = project(low, 256)
+
+        seg_here = seg_rows[b]
+        seg_before = jnp.where(b % blocks > 0, seg_rows[jnp.maximum(b - 1, 0)], -1)
+        seg_down = jnp.broadcast_to(seg_here, (BLOCK, BLOCK)).T
+        row = lax.broadcasted_iota(jnp.int32, (BLOCK, BLOCK), 0)
+        col = lax.broadcasted_iota(jnp.int32, (BLOCK, BLOCK), 1)
+        allowed = jnp.concatenate(
+            [
+                jnp.where(seg_down == seg_before, 1, 0),
+                jnp.where((seg_down == seg_here) & (col <= row), 1, 0),
+            ],
+            axis=1,
+        ) > 0
+        all_keys = keys[...]
+        all_values = values[...]
+        for h in range(cols // HEAD_DIM):
+            part = slice(h * HEAD_DIM, (h + 1) * HEAD_DIM)
+            scores = lax.dot_general(
+                query[:, part], all_keys, (((1,), (1,)), ((), ())),
+                preferred_element_type=jnp.float32,
+            ) * HEAD_DIM ** (-0.5)
+            scores = jnp.where(allowed, scores, masked_score)
+            powers = jnp.exp(scores - jnp.max(scores, axis=1, keepdims=True))
+            bottom = jnp.sum(powers, axis=1, keepdims=True)
+            context = jnp.dot(
+                powers.astype(jnp.bfloat16), all_values, preferred_element_type=jnp.float32
+            ) / bottom
+            context = context.astype(jnp.bfloat16).astype(jnp.float32)
+            result[b, :, part] = (got[b, 0, :, part].astype(jnp.float32) + context).astype(
+                jnp.bfloat16
+            )
+
+        rows = pl.ds(pl.multiple_of((b % blocks) * BLOCK, BLOCK), BLOCK)
+
+        @pl.when(b < blocks)
+        def _():
+            @pl.when(sec < sections - 1)
+            def _():
+                hand_copy(b).start()
+
+            pltpu.make_async_copy(result.at[b], out1_ref.at[0, rows], out_sem.at[b]).start()
+
+        @pl.when(b >= blocks)
+        def _():
+            pltpu.make_async_copy(result.at[b], out2_ref.at[0, rows], out_sem.at[b]).start()
+
+        down = b + 1 - late
+
+        @pl.when(middle & (down >= 1) & (down < blocks))
+        def _():
+            pass_down(down)
+
+        return carry
+
+    lax.fori_loop(0, steps, step, 0)
+
+    def drain(b, carry):
+        for way in range(2):
+            own_copy(got.at[b, 0], b, way).wait_send()
+            forward_copy(b, way).wait_send()
+        pltpu.make_async_copy(result.at[b], out1_ref.at[0, pl.ds(0, BLOCK)], out_sem.at[b]).wait()
+
+        @pl.when(b < blocks)
+        def _():
+            @pl.when(sec < sections - 1)
+            def _():
+                hand_copy(b).wait_send()
+
+            @pl.when(even & (sec > 0))
+            def _():
+                sum_copy(b).wait_send()
+
+        return carry
+
+    lax.fori_loop(0, steps, drain, 0)
+    for r in (1, 2, 3):
+        gain_copy(r).wait_send()
+
+    @pl.when(sec % 2 == 1)
+    def _():
+        mate_copy.wait_send()
+
+
+def relay(sections, activations, gain, w_query, w_kv, segments, pool, row_ids, row_lengths):
+    tokens, cols = activations.shape[1:]
+    blocks = tokens // BLOCK
+    steps = 2 * blocks
+    hosts_rows = pool.shape[0] * pool.shape[1]
+    dma = pltpu.SemaphoreType.DMA
+    bf16 = jnp.bfloat16
+    anywhere = pl.BlockSpec(memory_space=pl.ANY)
+    vmem = pl.BlockSpec(memory_space=pltpu.VMEM)
+    smem = pl.BlockSpec(memory_space=pltpu.SMEM)
+    return pl.pallas_call(
+        functools.partial(relay_kernel, sections, hosts_rows, row_ids.shape[0]),
+        out_shape=(
+            jax.ShapeDtypeStruct(activations.shape, bf16),
+            jax.ShapeDtypeStruct(activations.shape, bf16),
+        ),
+        in_specs=[anywhere, vmem, anywhere, anywhere, vmem, anywhere, smem, smem],
+        out_specs=(anywhere, anywhere),
+        scratch_shapes=[
+            pltpu.VMEM((steps, 4, BLOCK, cols), bf16),
+            pltpu.VMEM((4 * cols, cols + 2 * HEAD_DIM), bf16),
+            pltpu.VMEM((4, 2 * HEAD_DIM, cols), bf16),
+            pltpu.VMEM((4, 16, cols), bf16),
+            pltpu.VMEM((BLOCK, 4 * cols), bf16),
+            pltpu.VMEM((BLOCK, cols), bf16),
+            pltpu.VMEM((2 * BLOCK, HEAD_DIM), bf16),
+            pltpu.VMEM((2 * BLOCK, HEAD_DIM), bf16),
+            pltpu.VMEM((steps, 1, BLOCK), jnp.int32),
+            pltpu.VMEM((blocks, 1, BLOCK), jnp.int32),
+            pltpu.VMEM((2, *pool.shape), bf16),
+            pltpu.VMEM((blocks, BLOCK, cols), bf16),
+            pltpu.VMEM((blocks, BLOCK, cols), bf16),
+            pltpu.VMEM((steps, BLOCK, cols), bf16),
+            dma((steps, 2)), dma((steps, 2)), dma((steps, 2)), dma((steps, 2)),
+            dma((3,)), dma((3,)), dma((blocks,)), dma((blocks,)),
+            dma((blocks,)), dma((4,)), dma((4,)), dma, dma, dma,
+            dma((blocks,)), dma((blocks,)), dma((steps,)),
+        ],
+        compiler_params=pltpu.CompilerParams(
+            collective_id=0, has_side_effects=True, vmem_limit_bytes=48 * 1024 * 1024
+        ),
+    )(activations, gain, w_query, w_kv, segments, pool, row_ids, row_lengths)
+
+
 def solution(mesh):
+    square = (
+        mesh.shape["tensor"] == KV_HEADS == 4
+        and mesh.shape["section"] % 2 == 0
+        and mesh.shape["section"] >= 4
+    )
+    body = functools.partial(relay, mesh.shape["section"]) if square else per_device
     return jax.shard_map(
-        per_device,
+        body,
         mesh=mesh,
         in_specs=(
             P("section", None, "tensor"),

time: 235 us -> 92.9 us (0.40)
  waiting for transfers between devices: 121 us -> 0 us
  Pallas kernels: 0 us -> 83.4 us
  matrix products: 35 us -> 0 us
  other arithmetic: 27 us -> 0 us
  blocking collectives: 21.9 us -> 0 us
  between operations: 13.9 us -> 0.66 us
  local copies, waits for them, and re-layouts: 13.4 us -> 8.5 us
    all_gather x3 -> x0, waiting for transfers between devices: 121 us -> none  [the longest x2 103 us: attend(): part_cols = lax.all_gather(normed, 'tensor', axis=1, tiled=True)]
    pallas_call x0 -> x1, Pallas kernels: none -> 83.4 us  [relay(): pl.pallas_call(functools.partial(relay_kernel, sections, hosts_rows, row_...]
    dot_general x8 -> x0, matrix products: 35 us -> none  [the longest x2 14.1 us: attend(): jnp.dot(part_cols, query_weight, preferred_element_type=jnp.float32)]
    psum x2 -> x0, blocking collectives: 21.9 us -> none  [attend(): lax.psum(jnp.sum(wide_inputs * wide_inputs, axis=1), 'tensor')]
    sub x3 -> x0, other arithmetic: 11.4 us -> none  [the longest x2 11.4 us: attend(): weights = jax.nn.softmax(scores, axis=-1).astype(jnp.bfloat16)]
    convert_element_type x4 -> x0, other arithmetic: 9.62 us -> none  [the longest x2 5.83 us: attend(): return (wide_inputs + context.astype(jnp.float32)).astype(jnp.bfloat16)]
    unnamed x16, local copies, waits for them, and re-layouts: 1 us -> 8.5 us
    gather x1 -> x0, local copies, waits for them, and re-layouts: 6.21 us -> none  [pick_rows(): jnp.take(flat_rows, jnp.clip(source, 0, flat_rows.shape[0] - 1), axis=0)]
  transfers between devices with their start and end apart: 4 -> 0, of which waited for: 3 -> 0; matrix products, arithmetic and copies ran while one was open for 16% -> 0% of each run, Pallas kernels for 0% -> 0%
where the time goes in v1:
time: 92.9 us; the launch traced here: 92.6 us
  Pallas kernels  83.4 us (90%)
  local copies, waits for them, and re-layouts  8.5 us (9%)
    pallas_call x1, Pallas kernels, relay(): pl.pallas_call(functools.partial(relay_kernel, sections, hosts_rows, row_...  83.4 us
    unnamed x16, local copies, waits for them, and re-layouts  8.5 us

profile of v1, /device:TPU:0, one launch (start us, length us, event | category | flops | bytes accessed | tf_op | source)
XLA Modules:
  0.0 92.6 jit_solution(12272151809462192633)
XLA Ops:
  0.6 0.0 copy-start
  0.6 1.6 %copy-done = bf16[1,256,4096]{2,1,0:T(8,128)(2,1)S(1)} copy-done((bf16[1,256,4096]{2,1,0:T(8,128)(2,1)S(1)}, bf16[1,256,4096]{2,1,0:T(8,128)(2,1)}, u32[]{:S(2)}) %copy-start) | copy-done | bytes 2097176
  2.2 0.0 copy-start.1
  2.2 1.2 %copy-done.1 = bf16[1,512,1024]{2,1,0:T(8,128)(2,1)S(1)} copy-done((bf16[1,512,1024]{2,1,0:T(8,128)(2,1)S(1)}, bf16[1,512,1024]{2,1,0:T(8,128)(2,1)}, u32[]{:S(2)}) %copy-start.1) | copy-done | bytes 1048600
  3.5 0.0 copy-start.2
  3.5 1.0 %copy-done.2 = bf16[2,128,1024]{2,1,0:T(8,128)(2,1)S(1)} copy-done((bf16[2,128,1024]{2,1,0:T(8,128)(2,1)S(1)}, bf16[2,128,1024]{2,1,0:T(8,128)(2,1)}, u32[]{:S(2)}) %copy-start.2) | copy-done | bytes 524312
  4.5 0.0 copy-start.3
  4.5 0.7 copy-done.3
  5.2 0.0 copy-start.4
  5.2 0.7 copy-done.4
  5.9 0.0 copy-start.5
  5.9 0.7 copy-done.5
  6.6 0.0 copy-start.6
  6.6 0.7 copy-done.6
  7.2 83.4 %shard_map.95 = (bf16[1,512,1024]{2,1,0:T(8,128)(2,1)S(1)}, bf16[1,512,1024]{2,1,0:T(8,128)(2,1)S(1)}) custom-call(bf16[1,512,1024]{2,1,0:T(8,128)(2,1)S(1)} %copy-done.1, bf16[1,1024]{1,0:T(2,128)(2,1)S(1)} %copy-done.4, bf16[1,4096,1024]{2,1,0:T(8,128)(2,1)} %wq_ref.1, bf16[1,256,4096]{2,1,0:T(8,128)(2,1)S(1)} %copy-done, s32[8,512]{1,0:T(8,128)S(1)} %copy-done.3, ...), custom_call_target="tpu_custom_call" | custom-call | tf_op jit(solution)/shard_map/pallas_call | solution.py:455
  90.6 1.0 %copy.12 = bf16[1,512,1024]{2,1,0:T(8,128)(2,1)} copy(bf16[1,512,1024]{2,1,0:T(8,128)(2,1)S(1)} %get-tuple-element.4) | data formatting | bytes 2097152
  91.6 1.0 %copy.13 = bf16[1,512,1024]{2,1,0:T(8,128)(2,1)} copy(bf16[1,512,1024]{2,1,0:T(8,128)(2,1)S(1)} %get-tuple-element.5) | data formatting | bytes 2097152
Async XLA Ops:
  0.6 1.6 %copy-start = (bf16[1,256,4096]{2,1,0:T(8,128)(2,1)S(1)}, bf16[1,256,4096]{2,1,0:T(8,128)(2,1)}, u32[]{:S(2)}) copy-start(bf16[1,256,4096]{2,1,0:T(8,128)(2,1)} %wkv_ref.1) | copy-start | bytes 6291460
  2.2 1.2 %copy-start.1 = (bf16[1,512,1024]{2,1,0:T(8,128)(2,1)S(1)}, bf16[1,512,1024]{2,1,0:T(8,128)(2,1)}, u32[]{:S(2)}) copy-start(bf16[1,512,1024]{2,1,0:T(8,128)(2,1)} %a_ref.1) | copy-start | bytes 3145732
  3.5 1.0 %copy-start.2 = (bf16[2,128,1024]{2,1,0:T(8,128)(2,1)S(1)}, bf16[2,128,1024]{2,1,0:T(8,128)(2,1)}, u32[]{:S(2)}) copy-start(bf16[2,128,1024]{2,1,0:T(8,128)(2,1)} %pool_ref.1) | copy-start | bytes 1572868
  4.5 0.7 copy-start.3
  5.2 0.7 copy-start.4
  5.9 0.7 copy-start.5
  6.6 0.7 copy-start.6
